TPU v7x, 32 devices: a whole 2x2x4 slice. The times are simulated.
32 devices in a mesh: pool: 4 (over x, core), frame: 2 (over y), tensor: 4 (over z).
Axes of the slice: x: 2, y: 2, z: 4, core: 2. Of those that a mesh axis runs over, the one named last changes fastest.
Arguments:
- latents: bfloat16 [4096, 2240], P(('pool', 'frame', 'tensor')), parts along dimension 0, may hold values from -6 to 6
- queries: bfloat16 [4096, 2240], P(('pool', 'frame'), 'tensor'), parts along dimension 0, may hold values from -6 to 6
- keys: bfloat16 [4096, 2240], P(('pool', 'frame'), 'tensor'), parts along dimension 0, may hold values from -6 to 6
- values: bfloat16 [4096, 2240], P(('pool', 'frame'), 'tensor'), parts along dimension 0, may hold values from -6 to 6
- log_decay: float32 [20, 4096], P('tensor', ('pool', 'frame')), parts along dimension 1, may hold values from -0.6 to 0, as said below
- block_ids: int32 [4096], P(('pool', 'frame')), parts along dimension 0, may hold values from 0 to 3, as said below
- t_index: int32 [4], P('pool'), parts along dimension 0, may hold values from 0 to 49
- w_mod: bfloat16 [256, 8960], replicated, may hold values from -0.375 to 0.375
- w_out: bfloat16 [2240, 2240], P('tensor', 'frame'), may hold values from -0.125 to 0.125
- w_up: bfloat16 [2240, 4480], P('frame', 'tensor'), may hold values from -0.125 to 0.125
- w_down: bfloat16 [4480, 2240], P('tensor', 'frame'), may hold values from -0.09375 to 0.09375
Outputs:
- velocity: bfloat16 [4096, 2240], P(('pool', 'frame', 'tensor')), parts along dimension 0
- advanced: bfloat16 [4096, 2240], P(('pool', 'frame', 'tensor')), parts along dimension 0
There are 4 independent parts, one for each index of `pool`. A program takes and returns all parts, laid end to end along the dimension named above; an argument that names none is the same for every part. Nothing has to cross between parts.
Inputs may be any that keep to these rules, and one draw needn't show every extreme that they name: `block_ids`: within each span of 512 tokens the value never falls, starts at 0 and ends at 3. `log_decay`: every entry is negative.
All inputs are finite; a program needn't handle non-finite values.
Results may differ from a plain program's by a relative error of at most 0.0085.
Values may be sent and summed in bfloat16 or wider, within the bound.
A program may use at most 128 MiB of HBM per device.

v0:
```python
import functools
import math

import jax
import jax.numpy as jnp
from jax import lax
from jax.experimental import pallas as pl
from jax.experimental.pallas import tpu as pltpu
from jax.sharding import PartitionSpec as P

STEPS = 50


def shifted(block, axis, distance):
    devices = range(lax.axis_size(axis))
    route = [(i - distance, i) for i in devices if i - distance in devices]
    return lax.ppermute(block, axis, route)


def time_embedding(t_index, w_mod):
    fraction = 1.0 - t_index[0].astype(jnp.float32) / STEPS
    following = fraction - 1.0 / STEPS
    sigma_now = 3.0 * fraction / (1.0 + 2.0 * fraction)
    sigma_next = 3.0 * following / (1.0 + 2.0 * following)
    half_width = w_mod.shape[0] // 2
    frequency = jnp.exp(
        -math.log(10000.0) * jnp.arange(half_width).astype(jnp.float32) / half_width
    )
    angles = 1000.0 * sigma_now * frequency
    embedding = jnp.concatenate([jnp.cos(angles), jnp.sin(angles)])
    return (jax.nn.silu(embedding).astype(jnp.bfloat16), sigma_next - sigma_now)


def modulation_of(t_index, w_mod):
    time_features, step_size = time_embedding(t_index, w_mod)
    shifts = jnp.dot(time_features[None, :], w_mod, preferred_element_type=jnp.float32)[0]
    return (shifts, step_size)


def own_state(key_heads, value_heads, cumulative):
    block_total = cumulative[:, -1]
    scaled = key_heads.astype(jnp.float32) * jnp.exp(block_total[:, None] - cumulative)[:, :, None]
    state_sum = jnp.einsum(
        "htd,hte->hde", scaled, value_heads.astype(jnp.float32), precision=lax.Precision.HIGHEST
    )
    return (block_total, state_sum)


def mix_block(query_heads, key_heads, value_heads, cumulative, labels, carried_state):
    factor = query_heads.shape[2] ** (-0.5)
    visible = labels[None, :] <= labels[:, None]
    decay = jnp.exp(jnp.minimum(cumulative[:, :, None] - cumulative[:, None, :], 0.0))
    weights = jnp.where(visible[None], decay, 0.0) * factor
    scores = jnp.einsum("hid,hjd->hij", query_heads, key_heads, preferred_element_type=jnp.float32)
    probs = (scores * weights).astype(jnp.bfloat16)
    inner_part = jnp.einsum("hij,hjd->hid", probs, value_heads, preferred_element_type=jnp.float32)
    carried = jnp.einsum(
        "hid,hde->hie",
        query_heads.astype(jnp.float32),
        carried_state,
        precision=lax.Precision.HIGHEST,
    )
    numerator = inner_part + carried * (jnp.exp(cumulative) * factor)[:, :, None]
    normed = numerator * lax.rsqrt(jnp.mean(numerator * numerator, axis=2, keepdims=True) + 1e-06)
    return normed.astype(jnp.bfloat16)


def layer_norm(hidden):
    centered = hidden - jnp.mean(hidden, axis=1, keepdims=True)
    variance = jnp.mean(centered * centered, axis=1, keepdims=True)
    return centered * lax.rsqrt(variance + 1e-06)


def by_collectives(
    latents, queries, keys, values, log_decay, block_ids, t_index, w_mod, w_out, w_up, w_down
):
    shifts, step_size = modulation_of(t_index, w_mod)
    width = latents.shape[1]
    head_count = log_decay.shape[0]
    token_count = log_decay.shape[1]
    head_size = queries.shape[1] // head_count

    def to_heads(rows_in):
        return rows_in.reshape(token_count, head_count, head_size).transpose(1, 0, 2)

    query_heads = to_heads(queries)
    key_heads = to_heads(keys)
    value_heads = to_heads(values)
    cumulative = jnp.cumsum(log_decay, axis=1)
    block_total, state_sum = own_state(key_heads, value_heads, cumulative)
    keep_factor = jnp.exp(block_total)[:, None, None]

    def relay(turn, incoming):
        return shifted(
            (keep_factor * incoming + state_sum).astype(jnp.bfloat16), "frame", 1
        ).astype(jnp.float32)

    carried_state = lax.fori_loop(0, lax.axis_size("frame") - 1, relay, jnp.zeros_like(state_sum))
    mixed = mix_block(query_heads, key_heads, value_heads, cumulative, block_ids, carried_state)
    mixed_rows = mixed.transpose(1, 0, 2).reshape(token_count, head_count * head_size)
    head_terms = jnp.dot(
        mixed_rows,
        lax.all_gather(w_out, "frame", axis=1, tiled=True),
        preferred_element_type=jnp.float32,
    )
    attention = lax.psum_scatter(
        head_terms.astype(jnp.bfloat16), "tensor", scatter_dimension=0, tiled=True
    ).astype(jnp.float32)
    hidden = latents.astype(jnp.float32) + shifts[3 * width :] * attention
    normed = (layer_norm(hidden) * (1.0 + shifts[width : 2 * width]) + shifts[:width]).astype(
        jnp.bfloat16
    )
    normed_all = lax.all_gather(normed, "tensor", axis=0, tiled=True)
    up_sums = jnp.dot(
        normed_all,
        lax.all_gather(w_up, "frame", axis=0, tiled=True),
        preferred_element_type=jnp.float32,
    )
    units = jax.nn.gelu(up_sums, approximate=True).astype(jnp.bfloat16)
    unit_terms = jnp.dot(
        units,
        lax.all_gather(w_down, "frame", axis=1, tiled=True),
        preferred_element_type=jnp.float32,
    )
    feed = lax.psum_scatter(
        unit_terms.astype(jnp.bfloat16), "tensor", scatter_dimension=0, tiled=True
    ).astype(jnp.float32)
    velocity = (hidden + shifts[2 * width : 3 * width] * feed).astype(jnp.bfloat16)
    advanced = (latents.astype(jnp.float32) + step_size * velocity.astype(jnp.float32)).astype(
        jnp.bfloat16
    )
    return (velocity, advanced)


MESH = pl.DeviceIdType.MESH


def at_most(count, value):
    return jnp.minimum(jnp.maximum(value, 0), count - 1)


def fused(
    sizes,
    q_ref, k_ref, v_ref, decay_ref, label_ref, lat_ref, feature_ref,
    w_out_ref, w_up_ref, w_down_ref, w_mod_ref,
    velocity_ref,
    out_buf, up_buf, down_buf, mod_buf, state_out, state_in, mixed,
    first, first_in, spread, second, second_in, hidden, attended, units_own, columns, down_columns, key_rows, shift_rows,
    own_sem, y_send, y_recv, x_send, x_recv, core_send, core_recv, state_sems,
    first_send, first_recv, spread_send, spread_recv, second_send, second_recv,
):
    ranks, slabs, head_count, head_size, rows, tokens, quarters = sizes
    z = lax.axis_index("tensor")
    f = lax.axis_index("frame")
    pool = lax.axis_index("pool")
    core = lax.rem(pool, 2)
    other_core = pool + 1 - 2 * core
    other_chip = lax.rem(pool + 2, 4)
    other_f = 1 - f
    factor = head_size ** (-0.5)

    barrier = pltpu.get_barrier_semaphore()
    pl.semaphore_signal(barrier, inc=1, device_id={"frame": other_f}, device_id_type=MESH)
    pl.semaphore_signal(barrier, inc=1, device_id={"pool": other_core}, device_id_type=MESH)
    pl.semaphore_signal(barrier, inc=1, device_id={"pool": other_chip}, device_id_type=MESH)

    @pl.when(z > 0)
    def _():
        pl.semaphore_signal(barrier, inc=1, device_id={"tensor": z - 1}, device_id_type=MESH)

    @pl.when(z < ranks - 1)
    def _():
        pl.semaphore_signal(barrier, inc=1, device_id={"tensor": z + 1}, device_id_type=MESH)

    sources = (w_out_ref, w_up_ref, w_down_ref)
    buffers = (out_buf, up_buf, down_buf)
    own_copies = [
        pltpu.make_async_copy(sources[i], buffers[i].at[f], own_sem.at[i]) for i in range(3)
    ]
    for copy in own_copies:
        copy.start()
    mod_copy = pltpu.make_async_copy(w_mod_ref, mod_buf, own_sem.at[3])
    mod_copy.start()

    earlier = (
        lax.broadcasted_iota(jnp.int32, (tokens, tokens), 0)
        <= lax.broadcasted_iota(jnp.int32, (tokens, tokens), 1)
    ).astype(jnp.float32).astype(jnp.bfloat16)
    rest = decay_ref[...]
    cum = jnp.zeros_like(rest)
    for _ in range(3):
        leading = rest.astype(jnp.bfloat16)
        rest = rest - leading.astype(jnp.float32)
        cum += jnp.dot(leading, earlier, preferred_element_type=jnp.float32)
    columns[...] = jnp.zeros_like(columns)
    columns[0:head_count, :] = cum
    columns[head_count : head_count + 1, :] = label_ref[...].astype(jnp.float32)
    down_columns[...] = columns[...].T

    for h in range(head_count):
        part = slice(h * head_size, (h + 1) * head_size)
        row = cum[h : h + 1, :]
        total = row[:, tokens - 1 : tokens]
        keys = k_ref[part, :].astype(jnp.float32)
        key_rows[h] = keys.T.astype(jnp.bfloat16)
        scaled = (keys * jnp.exp(total - row)).astype(jnp.bfloat16)
        state_out[h] = lax.dot_general(
            v_ref[part, :], scaled, (((1,), (1,)), ((), ())), preferred_element_type=jnp.float32
        ).astype(jnp.bfloat16)

    links = 3 + (z > 0).astype(jnp.int32) + (z < ranks - 1).astype(jnp.int32)
    pl.semaphore_wait(barrier, links)

    state_copy = pltpu.make_async_remote_copy(
        src_ref=state_out, dst_ref=state_in, send_sem=state_sems.at[0], recv_sem=state_sems.at[1],
        device_id={"frame": other_f}, device_id_type=MESH,
    )

    @pl.when(f == 0)
    def _():
        state_copy.start()
        state_in[...] = jnp.zeros_like(state_in)

    def across(i, quarter):
        part = pl.ds(*quarters[i][quarter])
        return pltpu.make_async_remote_copy(
            src_ref=sources[i].at[part], dst_ref=buffers[i].at[f, part],
            send_sem=y_send.at[i], recv_sem=y_recv.at[i],
            device_id={"frame": other_f}, device_id_type=MESH,
        )

    def arrived(i, quarter):
        part = pl.ds(*quarters[i][quarter])
        return pltpu.make_async_remote_copy(
            src_ref=sources[i].at[part], dst_ref=buffers[i].at[other_f, part],
            send_sem=y_send.at[i], recv_sem=y_recv.at[i],
            device_id={"frame": other_f}, device_id_type=MESH,
        )

    def region(i, quarter):
        return buffers[i].at[other_f, pl.ds(*quarters[i][quarter])]

    def to_chip(i, quarter):
        return pltpu.make_async_remote_copy(
            src_ref=region(i, quarter), dst_ref=region(i, quarter),
            send_sem=x_send.at[i], recv_sem=x_recv.at[i],
            device_id={"pool": other_chip}, device_id_type=MESH,
        )

    def to_core(i, quarter, turn):
        return pltpu.make_async_remote_copy(
            src_ref=region(i, quarter), dst_ref=region(i, quarter),
            send_sem=core_send.at[i, turn], recv_sem=core_recv.at[i, turn],
            device_id={"pool": other_core}, device_id_type=MESH,
        )

    def each_quarter(act):
        for quarter in range(4):
            @pl.when(pool == quarter)
            def _():
                act(quarter)

    each_quarter(lambda quarter: across(0, quarter).start())

    def pass_on(i):
        def act(quarter):
            arrived(i, quarter).wait_recv()
            to_chip(i, quarter).start()
            to_core(i, quarter, 0).start()
        each_quarter(act)

    def pass_round(i):
        def act(quarter):
            opposite = (quarter + 2) % 4
            to_chip(i, opposite).wait_recv()
            to_core(i, opposite, 1).start()
        each_quarter(act)

    def settle(i):
        def act(quarter):
            to_core(i, quarter ^ 1, 0).wait_recv()
            to_core(i, (quarter ^ 1) ^ 2, 1).wait_recv()
        each_quarter(act)

    @pl.when(f > 0)
    def _():
        state_copy.wait_recv()

    def attend(d):
        block = pl.ds(pl.multiple_of(d * rows, rows), rows)
        visible = (
            down_columns[:, head_count : head_count + 1] <= columns[head_count : head_count + 1, block]
        )
        for h in range(head_count):
            part = slice(h * head_size, (h + 1) * head_size)
            qh = q_ref[part, block]
            scores = jnp.dot(key_rows[h], qh, preferred_element_type=jnp.float32)
            row = columns[h : h + 1, block]
            decay = jnp.exp(jnp.minimum(row - down_columns[:, h : h + 1], 0.0))
            probs = (scores * (jnp.where(visible, decay, 0.0) * factor)).astype(jnp.bfloat16)
            inner = jnp.dot(v_ref[part, :], probs, preferred_element_type=jnp.float32)
            carried = jnp.dot(state_in[h], qh, preferred_element_type=jnp.float32)
            numerator = inner + carried * (jnp.exp(row) * factor)
            power = jnp.mean(numerator * numerator, axis=0, keepdims=True)
            mixed[block, part] = (numerator * lax.rsqrt(power + 1e-06)).T.astype(jnp.bfloat16)

    own_copies[0].wait()

    def rows_of(d):
        return pl.ds(pl.multiple_of(d * rows, rows), rows)

    def hop(buf, landing, send_sem, recv_sem, way, d, s):
        to = at_most(ranks, z + 1 - 2 * way)
        return pltpu.make_async_remote_copy(
            src_ref=buf.at[d, s], dst_ref=landing.at[way, d, s],
            send_sem=send_sem.at[d, s], recv_sem=recv_sem.at[way, d, s],
            device_id={"tensor": to}, device_id_type=MESH,
        )

    def hop1(way, d, s):
        return hop(first, first_in, first_send, first_recv, way, d, s)

    shares = second_send.shape[2]

    def share(r):
        return pl.ds(r * (rows // shares), rows // shares)

    def hop2(way, d, s, r):
        to = at_most(ranks, z + 1 - 2 * way)
        return pltpu.make_async_remote_copy(
            src_ref=second.at[d, s, share(r)], dst_ref=second_in.at[way, d, s, share(r)],
            send_sem=second_send.at[d, s, r], recv_sem=second_recv.at[way, d, s, r],
            device_id={"tensor": to}, device_id_type=MESH,
        )

    def has_upstream(way):
        return jnp.where(way == 0, z > 0, z < ranks - 1)

    def first_turn(turn, s, fresh):
        step = turn // 2
        near = jnp.where(z < ranks // 2, 0, 1)
        way = lax.rem(turn + near, 2)
        d = jnp.where(way == 0, ranks - 1 - step, step)
        active = jnp.where(way == 0, d > z, d < z)

        @pl.when(active)
        def _():
            if fresh:
                attend(d)
            part = jnp.dot(mixed[rows_of(d), :], out_buf[s], preferred_element_type=jnp.float32)
            first[d, s] = part.astype(jnp.bfloat16)

            @pl.when(has_upstream(way))
            def _():
                hop1(way, d, s).wait_recv()
                first[d, s] = (
                    first[d, s].astype(jnp.float32) + first_in[way, d, s].astype(jnp.float32)
                ).astype(jnp.bfloat16)

            hop1(way, d, s).start()

    def own_slab(s):
        part = jnp.dot(mixed[rows_of(z), :], out_buf[s], preferred_element_type=jnp.float32)
        attended[s] = part.astype(jnp.bfloat16).astype(jnp.float32)

    def near_columns(turn, carry):
        first_turn(turn, f, True)

        @pl.when(turn == ranks // 2 - 1)
        def _():
            pass_on(0)
            each_quarter(lambda quarter: across(1, quarter).start())

        @pl.when(turn == ranks - 1)
        def _():
            pass_round(0)
            each_quarter(lambda quarter: across(2, quarter).start())

        return carry

    lax.fori_loop(0, 2 * (ranks - 1), near_columns, 0)
    attend(z)
    own_slab(f)
    settle(0)

    def far_columns(turn, carry):
        first_turn(turn, other_f, False)

        @pl.when(turn == 1)
        def _():
            pass_on(1)

        return carry

    lax.fori_loop(0, 2 * (ranks - 1), far_columns, 0)
    own_slab(other_f)

    mod_copy.wait()
    shift_rows[...] = jnp.dot(feature_ref[...], mod_buf[...], preferred_element_type=jnp.float32)
    piece = hidden.shape[2]

    def shift(kind, s):
        start = (kind * slabs + s) * piece
        return shift_rows[0:1, start : start + piece]

    def lat(s):
        return lat_ref[s * piece : (s + 1) * piece, :].astype(jnp.float32).T

    for way in range(2):
        @pl.when(has_upstream(way))
        def _():
            for s in range(slabs):
                hop1(way, z, s).wait_recv()
                attended[s] += first_in[way, z, s].astype(jnp.float32)

    total = jnp.zeros((rows, 1), jnp.float32)
    for s in range(slabs):
        value = lat(s) + shift(3, s) * attended[s]
        hidden[s] = value
        total += jnp.sum(value, axis=1, keepdims=True)
    width = slabs * hidden.shape[2]
    mean = total / width
    squares = jnp.zeros((rows, 1), jnp.float32)
    for s in range(slabs):
        centered = hidden[s] - mean
        squares += jnp.sum(centered * centered, axis=1, keepdims=True)
    inverse = lax.rsqrt(squares / width + 1e-06)
    for s in range(slabs):
        spread[z, s] = (
            (hidden[s] - mean) * inverse * (1.0 + shift(1, s)) + shift(0, s)
        ).astype(jnp.bfloat16)

    def relay(way, c, s):
        to = at_most(ranks, z + 1 - 2 * way)
        return pltpu.make_async_remote_copy(
            src_ref=spread.at[c, s], dst_ref=spread.at[c, s],
            send_sem=spread_send.at[way, c, s], recv_sem=spread_recv.at[c, s],
            device_id={"tensor": to}, device_id_type=MESH,
        )

    def has_downstream(way):
        return jnp.where(way == 0, z < ranks - 1, z > 0)

    for way in range(2):
        @pl.when(has_downstream(way))
        def _():
            for s in range(slabs):
                relay(way, z, s).start()

    pass_round(1)
    pass_on(2)
    own_copies[1].wait()
    settle(1)

    def up_side(c):
        acc = jnp.dot(spread[c, 0], up_buf[0], preferred_element_type=jnp.float32)
        for s in range(1, slabs):
            acc += jnp.dot(spread[c, s], up_buf[s], preferred_element_type=jnp.float32)
        return jax.nn.gelu(acc, approximate=True).astype(jnp.bfloat16)

    units_own[...] = up_side(z)

    def tick(k, carry):
        def chunk_of(way):
            return jnp.where(way == 0, z - k, z + k)

        def arrival(way, c0):
            c = chunk_of(way)

            @pl.when((c >= 0) & (c < ranks))
            def _():
                for s in range(slabs):
                    relay(way, c, s).wait_recv()

                    @pl.when(has_downstream(way))
                    def _():
                        relay(way, c, s).start()

            return c0

        def work(way, c0):
            c = chunk_of(way)

            @pl.when((c >= 0) & (c < ranks))
            def _():
                units = up_side(c)

                @pl.when((k == 1) & ((way == 0) | (z == 0)))
                def _():
                    own_copies[2].wait()
                    pass_round(2)
                    settle(2)

                for s in range(slabs):
                    second[c, s] = jnp.dot(
                        units, down_buf[s], preferred_element_type=jnp.float32
                    ).astype(jnp.bfloat16)

                    @pl.when(jnp.logical_not(has_upstream(1 - way)))
                    def _():
                        for r in range(shares):
                            hop2(1 - way, c, s, r).start()

            return c0

        @pl.when(k < ranks)
        def _():
            lax.fori_loop(0, 2, arrival, 0)
            lax.fori_loop(0, 2, work, 0)

        def sending(way, c0):
            place = jnp.where(way == 0, z, ranks - 1 - z)
            ahead = k - place
            d = jnp.where(way == 0, ahead, ranks - 1 - ahead)

            @pl.when((place > 0) & (ahead > place) & (ahead < ranks))
            def _():
                def slab(s, c1):
                    for r in range(shares):
                        hop2(way, d, s, r).wait_recv()
                        second[d, s, share(r)] = (
                            second[d, s, share(r)].astype(jnp.float32)
                            + second_in[way, d, s, share(r)].astype(jnp.float32)
                        ).astype(jnp.bfloat16)
                        hop2(way, d, s, r).start()
                    return c1

                lax.fori_loop(0, slabs, slab, 0)

            return c0

        lax.fori_loop(0, 2, sending, 0)
        return carry

    lax.fori_loop(1, 2 * ranks - 2, tick, 0)

    for s in range(slabs):
        attended[s] = (
            jnp.dot(units_own[...], down_buf[s], preferred_element_type=jnp.float32)
            .astype(jnp.bfloat16)
            .astype(jnp.float32)
        )
    for way in range(2):
        @pl.when(has_upstream(way))
        def _():
            for s in range(slabs):
                for r in range(shares):
                    hop2(way, z, s, r).wait_recv()
                attended[s] += second_in[way, z, s].astype(jnp.float32)
    for s in range(slabs):
        velocity = hidden[s] + shift(2, s) * attended[s]
        velocity_ref[s * piece : (s + 1) * piece, :] = velocity.T

    @pl.when(f == 0)
    def _():
        state_copy.wait_send()

    for i in range(3):
        def left(quarter):
            across(i, quarter).wait_send()
            to_chip(i, quarter).wait_send()
            to_core(i, quarter, 0).wait_send()
            to_core(i, (quarter + 2) % 4, 1).wait_send()
        each_quarter(left)

    def drain(d, carry):
        def slab(s, c):
            @pl.when(d != z)
            def _():
                way = jnp.where(d > z, 0, 1)
                hop1(way, d, s).wait_send()
                for r in range(shares):
                    hop2(way, d, s, r).wait_send()

            def direction(way, c1):
                came = jnp.where(way == 0, d <= z, d >= z)

                @pl.when(came & has_downstream(way))
                def _():
                    relay(way, d, s).wait_send()

                return c1

            lax.fori_loop(0, 2, direction, 0)
            return c

        lax.fori_loop(0, slabs, slab, 0)
        return carry

    lax.fori_loop(0, ranks, drain, 0)


def fits(latents, queries, log_decay, w_out, w_up, w_down):
    frames, ranks, pools = (lax.axis_size(a) for a in ("frame", "tensor", "pool"))
    rows, tokens = latents.shape[0], queries.shape[0]
    return (
        frames == 2
        and pools == 4
        and ranks > 1
        and rows % 128 == 0
        and latents.shape[1] % (16 * frames) == 0
        and log_decay.shape[0] < 8
        and rows * ranks == tokens
        and rows % 16 == 0
        and all(w.shape[0] % 16 == 0 and w.shape[0] >= 64 for w in (w_out, w_up, w_down))
        and w_up.shape[0] == w_out.shape[1] == w_down.shape[1]
        and queries.shape[1] // log_decay.shape[0] % 16 == 0
    )


def on_device(
    latents, queries, keys, values, log_decay, block_ids, t_index, w_mod, w_out, w_up, w_down
):
    if not fits(latents, queries, log_decay, w_out, w_up, w_down):
        return by_collectives(
            latents, queries, keys, values, log_decay, block_ids, t_index, w_mod, w_out, w_up, w_down
        )
    ranks, slabs = lax.axis_size("tensor"), lax.axis_size("frame")
    rows, width = latents.shape
    piece = width // slabs
    tokens, features = queries.shape
    head_count = log_decay.shape[0]
    head_size = features // head_count
    time_features, step_size = time_embedding(t_index, w_mod)

    def split(count):
        edges = [count // 16 * i // 4 * 16 for i in range(5)]
        return tuple((edges[i], edges[i + 1] - edges[i]) for i in range(4))

    quarters = tuple(split(w.shape[0]) for w in (w_out, w_up, w_down))
    sizes = (ranks, slabs, head_count, head_size, rows, tokens, quarters)
    block = (ranks, slabs, rows, piece)
    vmem = pl.BlockSpec(memory_space=pltpu.VMEM)
    anywhere = pl.BlockSpec(memory_space=pl.ANY)
    dma = pltpu.SemaphoreType.DMA
    velocity = pl.pallas_call(
        functools.partial(fused, sizes),
        out_shape=jax.ShapeDtypeStruct((width, rows), jnp.float32),
        in_specs=[vmem] * 7 + [anywhere] * 4,
        out_specs=vmem,
        scratch_shapes=[
            pltpu.VMEM((slabs,) + w_out.shape, jnp.bfloat16),
            pltpu.VMEM((slabs,) + w_up.shape, jnp.bfloat16),
            pltpu.VMEM((slabs,) + w_down.shape, jnp.bfloat16),
            pltpu.VMEM(w_mod.shape, jnp.bfloat16),
            pltpu.VMEM((head_count, head_size, head_size), jnp.bfloat16),
            pltpu.VMEM((head_count, head_size, head_size), jnp.bfloat16),
            pltpu.VMEM((tokens, features), jnp.bfloat16),
            pltpu.VMEM(block, jnp.bfloat16),
            pltpu.VMEM((2,) + block, jnp.bfloat16),
            pltpu.VMEM(block, jnp.bfloat16),
            pltpu.VMEM(block, jnp.bfloat16),
            pltpu.VMEM((2,) + block, jnp.bfloat16),
            pltpu.VMEM((slabs, rows, piece), jnp.float32),
            pltpu.VMEM((slabs, rows, piece), jnp.float32),
            pltpu.VMEM((rows, w_up.shape[1]), jnp.bfloat16),
            pltpu.VMEM((8, tokens), jnp.float32),
            pltpu.VMEM((tokens, 8), jnp.float32),
            pltpu.VMEM((head_count, tokens, head_size), jnp.bfloat16),
            pltpu.VMEM((8, w_mod.shape[1]), jnp.float32),
            dma((4,)), dma((3,)), dma((3,)), dma((3,)), dma((3,)), dma((3, 2)), dma((3, 2)), dma((2,)),
            dma((ranks, slabs)), dma((2, ranks, slabs)),
            dma((2, ranks, slabs)), dma((ranks, slabs)),
            dma((ranks, slabs, 4)), dma((2, ranks, slabs, 4)),
        ],
        compiler_params=pltpu.CompilerParams(
            collective_id=0, has_side_effects=True, vmem_limit_bytes=56 * 1024 * 1024
        ),
        name="sublayers",
    )(
        queries.T, keys.T, values.T, log_decay, block_ids[None, :], latents.T,
        jnp.broadcast_to(time_features, (8, time_features.shape[0])),
        w_out, w_up, w_down, w_mod,
    )
    velocity = velocity.T.astype(jnp.bfloat16)
    advanced = latents.astype(jnp.float32) + step_size * velocity.astype(jnp.float32)
    return (velocity, advanced.astype(jnp.bfloat16))


def solution(mesh):
    return jax.shard_map(
        on_device,
        mesh=mesh,
        in_specs=(
            P(("pool", "frame", "tensor"), None),
            P(("pool", "frame"), "tensor"),
            P(("pool", "frame"), "tensor"),
            P(("pool", "frame"), "tensor"),
            P("tensor", ("pool", "frame")),
            P(("pool", "frame")),
            P("pool"),
            P(),
            P("tensor", "frame"),
            P("frame", "tensor"),
            P("tensor", "frame"),
        ),
        out_specs=(P(("pool", "frame", "tensor"), None), P(("pool", "frame", "tensor"), None)),
        check_vma=False,
    )
```

profile of v0, /device:TPU:29, one launch (start us, length us, event | category | flops | bytes accessed | tf_op | source)
XLA Modules:
  0.0 135.2 jit_solution(13863390564376146893)
XLA Ops:
  1.4 0.6 broadcast_in_dim.7.feature_ref
  2.0 0.0 copy-start
  2.0 130.7 %sublayers.1 = f32[2240,128]{1,0:T(8,128)} custom-call(bf16[560,512]{1,0:T(8,128)(2,1)} %bitcast.11, bf16[560,512]{1,0:T(8,128)(2,1)} %bitcast.12, bf16[560,512]{1,0:T(8,128)(2,1)} %bitcast.13, f32[5,512]{1,0:T(8,128)} %decay_ref.1, s32[1,512]{1,0:T(1,128)} %bitcast.14, bf16[2240,128]{1,0:T(8,128)(2,1)} %bitcast.10, ...), custom_call_target="tpu_custom_call" | custom-call | tf_op jit(solution)/shard_map/sublayers/pallas_call | solution.py:636
  132.7 0.0 copy-done
  132.8 2.4 %add_convert_fusion = (bf16[128,2240]{0,1:T(8,128)(2,1)}, bf16[128,2240]{0,1:T(8,128)(2,1)}) fusion(bf16[128,2240]{0,1:T(8,128)(2,1)S(1)} %copy-done, f32[]{:T(128)} %bitcast.7, f32[2240,128]{1,0:T(8,128)} %sublayers.1), kind=kLoop, calls=%fused_computation | loop fusion | flops 1720320 | bytes 2867204 | tf_op jit(solution)/shard_map/convert_element_type | solution.py:677
  (2 shorter events, 0.1 us)
Async XLA Ops:
  2.0 130.7 %copy-start = (bf16[128,2240]{0,1:T(8,128)(2,1)S(1)}, bf16[128,2240]{0,1:T(8,128)(2,1)}, u32[]{:S(2)}) copy-start(bf16[128,2240]{0,1:T(8,128)(2,1)} %param.11) | copy-start | bytes 1720324
where the time goes:
time: 135 us
  Pallas kernels  131 us (97%)
  other arithmetic  2.51 us (2%)
  between operations  1.39 us (1%)
    pallas_call x1, Pallas kernels, on_device(): pl.pallas_call(functools.partial(fused, sizes), out_shape=jax.ShapeDtypeS...  131 us

commit v1 on v0

--- a/solution.py
+++ b/solution.py
@@ -464,17 +464,17 @@
         def chunk_of(way):
             return jnp.where(way == 0, z - k, z + k)
 
-        def arrival(way, c0):
+        def arrival(turn, c0):
+            s, way = turn // 2, lax.rem(turn, 2)
             c = chunk_of(way)
 
             @pl.when((c >= 0) & (c < ranks))
             def _():
-                for s in range(slabs):
-                    relay(way, c, s).wait_recv()
-
-                    @pl.when(has_downstream(way))
-                    def _():
-                        relay(way, c, s).start()
+                relay(way, c, s).wait_recv()
+
+                @pl.when(has_downstream(way))
+                def _():
+                    relay(way, c, s).start()
 
             return c0
 
@@ -505,7 +505,7 @@
 
         @pl.when(k < ranks)
         def _():
-            lax.fori_loop(0, 2, arrival, 0)
+            lax.fori_loop(0, 2 * slabs, arrival, 0)
             lax.fori_loop(0, 2, work, 0)
 
         def sending(way, c0):

time: 135 us -> 135 us (level)
  no operation moved by 1% of the time
where the time goes in v1:
time: 135 us
  Pallas kernels  131 us (97%)
  other arithmetic  2.51 us (2%)
  between operations  1.39 us (1%)
    pallas_call x1, Pallas kernels, on_device(): pl.pallas_call(functools.partial(fused, sizes), out_shape=jax.ShapeDtypeS...  131 us

profile of v1, /device:TPU:29, one launch (start us, length us, event | category | flops | bytes accessed | tf_op | source)
XLA Modules:
  0.0 135.2 jit_solution(10800424668851227458)
XLA Ops:
  1.4 0.6 broadcast_in_dim.7.feature_ref
  2.0 0.0 copy-start
  2.0 130.7 %sublayers.1 = f32[2240,128]{1,0:T(8,128)} custom-call(bf16[560,512]{1,0:T(8,128)(2,1)} %bitcast.11, bf16[560,512]{1,0:T(8,128)(2,1)} %bitcast.12, bf16[560,512]{1,0:T(8,128)(2,1)} %bitcast.13, f32[5,512]{1,0:T(8,128)} %decay_ref.1, s32[1,512]{1,0:T(1,128)} %bitcast.14, bf16[2240,128]{1,0:T(8,128)(2,1)} %bitcast.10, ...), custom_call_target="tpu_custom_call" | custom-call | tf_op jit(solution)/shard_map/sublayers/pallas_call | solution.py:636
  132.7 0.0 copy-done
  132.7 2.4 %add_convert_fusion = (bf16[128,2240]{0,1:T(8,128)(2,1)}, bf16[128,2240]{0,1:T(8,128)(2,1)}) fusion(bf16[128,2240]{0,1:T(8,128)(2,1)S(1)} %copy-done, f32[]{:T(128)} %bitcast.7, f32[2240,128]{1,0:T(8,128)} %sublayers.1), kind=kLoop, calls=%fused_computation | loop fusion | flops 1720320 | bytes 2867204 | tf_op jit(solution)/shard_map/convert_element_type | solution.py:677
  (2 shorter events, 0.1 us)
Async XLA Ops:
  2.0 130.7 %copy-start = (bf16[128,2240]{0,1:T(8,128)(2,1)S(1)}, bf16[128,2240]{0,1:T(8,128)(2,1)}, u32[]{:S(2)}) copy-start(bf16[128,2240]{0,1:T(8,128)(2,1)} %param.11) | copy-start | bytes 1720324
